TPU v7x, 512 devices: a whole 4x4x16 slice. The times are simulated.
512 devices in a mesh: seq: 32 (over z, core), mem: 16 (over y, x).
Axes of the slice: x: 4, y: 4, z: 16, core: 2. Of those that a mesh axis runs over, the one named last changes fastest.
Arguments:
- queries: bfloat16 [65536, 1024], P(('seq', 'mem'))
- local_keys: bfloat16 [65536, 1024], P(('seq', 'mem'))
- local_values: bfloat16 [65536, 1024], P(('seq', 'mem')), may hold values from -6 to 6
- memory_keys: bfloat16 [8192, 1024], P('mem')
- memory_values: bfloat16 [8192, 1024], P('mem'), may hold values from -6 to 6
- block_lists: int32 [1024, 8], P('seq'), may hold values from 0 to 127, as said below
- block_counts: int32 [1024], P('seq'), may hold values from 1 to 8
- doc_starts: int32 [4], replicated, may hold values from 0 to 65024, as said below
- gate_bias: float32 [8], replicated, may hold values from -2 to 2
Outputs:
- attended: bfloat16 [65536, 1024], P(('seq', 'mem'))
Inputs may be any that keep to these rules, and one draw needn't show every extreme that they name: `block_lists`: slots at or past a query block's count are padding; a block may stand in several slots of one list. Query block i lists only blocks of shards o with o % 2 == (i + i // 2) % 2, and its slot 0 names a block of shard (i + i // 2) % 2; so of the 2 query blocks of one device, at most 1 lists blocks of a given shard (the other never does); for shard (i + i // 2) % 2 that block surely does, for other shards possibly none does. `doc_starts`: the first entry is 0; the entries do not fall (equal ones allowed); the last entry is 65024.
All inputs are finite; a program needn't handle non-finite values.
Results may differ from a plain program's by a relative error of at most 0.0105.
Values may be sent and summed in bfloat16 or wider, within the bound.
A program may use at most 64 MiB of HBM per device.

v0:
```python
import jax
import jax.numpy as jnp
from jax import lax
from jax.sharding import PartitionSpec as P

WINDOW = 1024
QBLK = 64
MBLK = 64
LIST = 8


def from_behind(block, axis, distance):
    devices = range(lax.axis_size(axis))
    route = [(i - distance, i) for i in devices if i - distance in devices]
    return lax.ppermute(block, axis, route)


def row_hits(lists, counts, owner_index, blocks_here):
    slot_live = jnp.arange(LIST, dtype=jnp.int32)[None, :] < counts[:, None]
    local_ids = lists - owner_index * blocks_here
    block_hit = jnp.any(
        slot_live[:, :, None]
        & (local_ids[:, :, None] == jnp.arange(blocks_here, dtype=jnp.int32)[None, None, :]),
        axis=1,
    )
    return jnp.repeat(jnp.repeat(block_hit, QBLK, axis=0), MBLK, axis=1)


def owner_work(query_rows, row_hit, memory_keys, memory_values, head_count, head_size, score_scale):
    all_rows = query_rows.shape[0]
    mem_rows = memory_keys.shape[0]
    query_heads = query_rows.reshape(all_rows, head_count, head_size).transpose(1, 0, 2)
    key_heads = memory_keys.reshape(mem_rows, head_count, head_size).transpose(1, 0, 2)
    value_heads = memory_values.reshape(mem_rows, head_count, head_size).transpose(1, 0, 2)

    def owner_partial(operands):
        query_head, key_head, value_head = operands
        scores = (
            jnp.einsum("qd,kd->qk", query_head, key_head, preferred_element_type=jnp.float32)
            * score_scale
        )
        scores = jnp.where(row_hit, scores, -1e30)
        maxima = jnp.max(scores, axis=1)
        weights = jnp.where(row_hit, jnp.exp(scores - maxima[:, None]), 0.0)
        totals = jnp.sum(weights, axis=1)
        numerator = jnp.dot(
            weights.astype(jnp.bfloat16), value_head, preferred_element_type=jnp.float32
        )
        readout = (numerator / jnp.where(totals > 0, totals, 1.0)[:, None]).astype(jnp.bfloat16)
        return (readout, maxima, totals)

    return lax.map(owner_partial, (query_heads, key_heads, value_heads))


def send_back(readouts, maxima, totals):
    received = lax.all_to_all(readouts, "mem", split_axis=1, concat_axis=1, tiled=True).astype(
        jnp.float32
    )
    got_max, got_total = (
        lax.all_to_all(maxima, "mem", split_axis=1, concat_axis=1, tiled=True),
        lax.all_to_all(totals, "mem", split_axis=1, concat_axis=1, tiled=True),
    )
    return (received, got_max, got_total)


def combine(received, got_max, got_total):
    largest = jnp.max(got_max, axis=1)
    shares = got_total * jnp.exp(got_max - largest[:, None, :])
    return jnp.sum(shares[..., None] * received, axis=1) / jnp.sum(shares, axis=1)[..., None]


def on_device(
    queries,
    local_keys,
    local_values,
    memory_keys,
    memory_values,
    block_lists,
    block_counts,
    doc_starts,
    gate_bias,
):
    tok_rows = queries.shape[0]
    model_width = queries.shape[1]
    head_count = gate_bias.shape[0]
    head_size = model_width // head_count
    score_scale = float(head_size) ** (-0.5)
    group_size = lax.axis_size("mem")
    owner_index = lax.axis_index("mem")
    device_index = lax.axis_index(("seq", "mem"))
    reach_shards = WINDOW // tok_rows
    blocks_here = memory_keys.shape[0] // MBLK
    gathered = lax.all_gather(queries, "mem", axis=0, tiled=True)
    row_hit = row_hits(block_lists, block_counts, owner_index, blocks_here)
    readouts, maxima, totals = owner_work(
        gathered, row_hit, memory_keys, memory_values, head_count, head_size, score_scale
    )
    received, got_max, got_total = send_back(
        readouts.reshape(head_count, group_size, tok_rows, head_size),
        maxima.reshape(head_count, group_size, tok_rows),
        totals.reshape(head_count, group_size, tok_rows),
    )
    memory_out = combine(received, got_max, got_total)
    key_parts = [local_keys]
    value_parts = [local_values]
    for distance in range(1, reach_shards + 1):
        came_keys, came_values = from_behind((local_keys, local_values), ("seq", "mem"), distance)
        key_parts.insert(0, came_keys)
        value_parts.insert(0, came_values)
    window_keys = jnp.concatenate(key_parts, axis=0)
    window_values = jnp.concatenate(value_parts, axis=0)
    window_rows = window_keys.shape[0]
    row_base = device_index * tok_rows
    query_pos = row_base + jnp.arange(tok_rows, dtype=jnp.int32)
    key_pos = row_base - reach_shards * tok_rows + jnp.arange(window_rows, dtype=jnp.int32)
    doc_first = jnp.max(
        jnp.where(doc_starts[None, :] <= query_pos[:, None], doc_starts[None, :], 0), axis=1
    )
    visible = (
        (key_pos[None, :] <= query_pos[:, None])
        & (query_pos[:, None] - key_pos[None, :] < WINDOW)
        & (key_pos[None, :] >= doc_first[:, None])
    )
    query_three = queries.reshape(tok_rows, head_count, head_size)
    key_three = window_keys.reshape(window_rows, head_count, head_size)
    value_three = window_values.reshape(window_rows, head_count, head_size)
    local_scores = (
        jnp.einsum("qhd,khd->hqk", query_three, key_three, preferred_element_type=jnp.float32)
        * score_scale
    )
    local_max = jnp.max(jnp.where(visible[None], local_scores, -1e30), axis=-1)
    local_weights = jnp.where(visible[None], jnp.exp(local_scores - local_max[..., None]), 0.0)
    local_total = jnp.sum(local_weights, axis=-1)
    local_out = (
        jnp.einsum(
            "hqk,khd->hqd",
            local_weights.astype(jnp.bfloat16),
            value_three,
            preferred_element_type=jnp.float32,
        )
        / local_total[..., None]
    )
    gate_share = jax.nn.sigmoid(gate_bias)[:, None, None]
    mixed = gate_share * memory_out + (1.0 - gate_share) * local_out
    return jnp.transpose(mixed, (1, 0, 2)).reshape(tok_rows, model_width).astype(jnp.bfloat16)


def solution(mesh):
    in_specs = (
        P(("seq", "mem"), None),
        P(("seq", "mem"), None),
        P(("seq", "mem"), None),
        P("mem", None),
        P("mem", None),
        P("seq", None),
        P("seq"),
        P(),
        P(),
    )
    out_specs = P(("seq", "mem"), None)
    return jax.shard_map(
        on_device, mesh=mesh, in_specs=in_specs, out_specs=out_specs, check_vma=False
    )
```

profile of v0, /device:TPU:40, one launch (start us, length us, event | category | flops | bytes accessed | tf_op | source)
XLA Modules:
  0.0 329.1 jit_solution(3787371529237754044)
XLA Ops:
  6.5 1.9 copy.85
  9.6 4.2 %collective-permute-start = (bf16[128,1024]{0,1:T(8,128)(2,1)S(1)}, bf16[128,1024]{0,1:T(8,128)(2,1)}, u32[]{:S(2)}, u32[]{:S(2)}) collective-permute-start(bf16[128,1024]{0,1:T(8,128)(2,1)S(1)} %copy.94), channel_id=1, source_target_pairs={{0,8},{1,9},{2,10},{3,11},{4,12},{5,13},{6,14},{7,15},{8,16},{9,17... | collective-permute-start | bytes 786440 | tf_op jit(solution)/shard_map/ppermute | solution.py:15
  13.8 3.4 %collective-permute-start.1 = (bf16[128,1024]{0,1:T(8,128)(2,1)S(1)}, bf16[128,1024]{0,1:T(8,128)(2,1)}, u32[]{:S(2)}, u32[]{:S(2)}) collective-permute-start(bf16[128,1024]{0,1:T(8,128)(2,1)S(1)} %copy.94), channel_id=1, source_target_pairs={{0,7},{1,8},{2,9},{3,10},{4,11},{5,12},{6,13},{7,14},{8,15},{9,16}... | collective-permute-start | bytes 786440 | tf_op jit(solution)/shard_map/ppermute | solution.py:15
  17.2 5.2 %collective-permute-start.8 = (bf16[128,1024]{1,0:T(8,128)(2,1)}, bf16[128,1024]{1,0:T(8,128)(2,1)}, u32[]{:S(2)}, u32[]{:S(2)}) collective-permute-start(bf16[128,1024]{1,0:T(8,128)(2,1)} %param.13), channel_id=1, source_target_pairs={{0,8},{1,9},{2,10},{3,11},{4,12},{5,13},{6,14},{7,15},{8,16},{9,17... | collective-permute-start | bytes 786440 | tf_op jit(solution)/shard_map/ppermute | solution.py:15
  22.4 3.5 %collective-permute-start.9 = (bf16[128,1024]{1,0:T(8,128)(2,1)}, bf16[128,1024]{1,0:T(8,128)(2,1)}, u32[]{:S(2)}, u32[]{:S(2)}) collective-permute-start(bf16[128,1024]{1,0:T(8,128)(2,1)} %param.13), channel_id=1, source_target_pairs={{0,7},{1,8},{2,9},{3,10},{4,11},{5,12},{6,13},{7,14},{8,15},{9,16}... | collective-permute-start | bytes 786440 | tf_op jit(solution)/shard_map/ppermute | solution.py:15
  25.9 5.0 %collective-permute-start.10 = (bf16[128,1024]{1,0:T(8,128)(2,1)}, bf16[128,1024]{1,0:T(8,128)(2,1)}, u32[]{:S(2)}, u32[]{:S(2)}) collective-permute-start(bf16[128,1024]{1,0:T(8,128)(2,1)} %param.13), channel_id=1, source_target_pairs={{0,6},{1,7},{2,8},{3,9},{4,10},{5,11},{6,12},{7,13},{8,14},{9,15},... | collective-permute-start | bytes 786440 | tf_op jit(solution)/shard_map/ppermute | solution.py:15
  32.6 1.5 copy.86
  34.7 62.9 %all-gather.2.cloned.1.call-done = bf16[2048,1024]{0,1:T(8,128)(2,1)} async-done(((bf16[128,1024]{0,1:T(8,128)(2,1)}), bf16[2048,1024]{0,1:T(8,128)(2,1)}) %all-gather.2.cloned.1.call-update) | async-done | bytes 4194320 | tf_op jit(solution)/shard_map/all_gather | solution.py:93
  97.7 61.5 %while.15 = (s32[]{:T(128)}, bf16[8,2048,128]{2,1,0:T(8,128)(2,1)}, f32[8,2048]{1,0:T(8,128)}, f32[8,2048]{1,0:T(8,128)}, bf16[8,2048,128]{1,2,0:T(8,128)(2,1)},...) while((s32[]{:T(128)}, bf16[8,2048,128]{2,1,0:T(8,128)(2,1)}, ...), condition=%wide.region_4.5_spmd.clone, body=%wide.region_1.4_spmd.clone.sunk | while | flops 546832384 | bytes 14010477 | solution.py:52
  97.7 1.9 fusion.64
  100.7 1.7 fusion.66
  105.4 1.9 fusion.64
  108.4 1.7 fusion.66
  113.0 1.9 fusion.64
  116.0 1.7 fusion.66
  120.7 1.9 fusion.64
  123.7 1.7 fusion.66
  128.4 1.9 fusion.64
  131.4 1.7 fusion.66
  136.1 1.9 fusion.64
  139.1 1.7 fusion.66
  143.8 1.9 fusion.64
  146.8 1.7 fusion.66
  151.4 1.9 fusion.64
  154.4 1.8 fusion.66
  159.2 5.8 %all-to-all-start.1 = ((f32[8,16,128]{2,0,1:T(8,128)}), f32[8,16,128]{2,0,1:T(8,128)S(1)}, u32[]{:S(2)}, u32[]{:S(2)}) async-start(f32[8,16,128]{2,0,1:T(8,128)} %bitcast.7), calls=%async_computation.1 | async-start | bytes 131072 | tf_op jit(solution)/shard_map/all_to_all | solution.py:60
  164.9 6.3 %all-to-all-done.1 = f32[8,16,128]{2,0,1:T(8,128)S(1)} async-done(((f32[8,16,128]{2,0,1:T(8,128)}), f32[8,16,128]{2,0,1:T(8,128)S(1)}, u32[]{:S(2)}, u32[]{:S(2)}) %all-to-all-start.1) | async-done | bytes 65568 | tf_op jit(solution)/shard_map/all_to_all | solution.py:60
  171.2 4.8 %all-to-all-start = ((f32[8,16,128]{2,0,1:T(8,128)}), f32[8,16,128]{2,0,1:T(8,128)S(1)}, u32[]{:S(2)}, u32[]{:S(2)}) async-start(f32[8,16,128]{2,0,1:T(8,128)} %bitcast.6), calls=%async_computation | async-start | bytes 131072 | tf_op jit(solution)/shard_map/all_to_all | solution.py:61
  176.1 4.7 %copy.91 = bf16[8,16,128,128]{3,2,0,1:T(8,128)(2,1)} copy(bf16[8,16,128,128]{3,2,1,0:T(8,128)(2,1)} %bitcast.107) | data formatting | bytes 8388608 | tf_op jit(solution)/shard_map/reshape | solution.py:99
  180.8 1.5 all-to-all-done
  182.3 5.9 %all-to-all-start.2 = ((bf16[8,16,128,128]{3,2,0,1:T(8,128)(2,1)}), bf16[8,16,128,128]{3,2,0,1:T(8,128)(2,1)}, u32[]{:S(2)}, u32[]{:S(2)}) async-start(bf16[8,16,128,128]{3,2,0,1:T(8,128)(2,1)} %copy.91), calls=%async_computation.2 | async-start | bytes 8388608 | tf_op jit(solution)/shard_map/all_to_all | solution.py:56
  188.5 4.3 %collective-permute-start.11 = (bf16[128,1024]{1,0:T(8,128)(2,1)S(1)}, bf16[128,1024]{1,0:T(8,128)(2,1)S(1)}, u32[]{:S(2)}, u32[]{:S(2)}) collective-permute-start(bf16[128,1024]{1,0:T(8,128)(2,1)S(1)} %copy-done.4), channel_id=1, source_target_pairs={{0,5},{1,6},{2,7},{3,8},{4,9},{5,10},{6,11},{7,12},{8,13},{9,14},{... | collective-permute-start | bytes 786440 | tf_op jit(solution)/shard_map/ppermute | solution.py:15
  193.8 3.1 collective-permute-start.12
  197.9 3.1 collective-permute-start.13
  202.0 39.1 %collective-permute-done.11 = bf16[128,1024]{1,0:T(8,128)(2,1)S(1)} collective-permute-done((bf16[128,1024]{1,0:T(8,128)(2,1)S(1)}, bf16[128,1024]{1,0:T(8,128)(2,1)S(1)}, u32[]{:S(2)}, u32[]{:S(2)}) %collective-permute-start.11) | collective-permute-done | bytes 262176 | tf_op jit(solution)/shard_map/ppermute | solution.py:15
  241.1 8.3 %collective-permute-start.14 = (bf16[128,1024]{1,0:T(8,128)(2,1)S(1)}, bf16[128,1024]{1,0:T(8,128)(2,1)S(1)}, u32[]{:S(2)}, u32[]{:S(2)}) collective-permute-start(bf16[128,1024]{1,0:T(8,128)(2,1)S(1)} %copy-done.4), channel_id=1, source_target_pairs={{0,2},{1,3},{2,4},{3,5},{4,6},{5,7},{6,8},{7,9},{8,10},{9,11},{10,... | collective-permute-start | bytes 786440 | tf_op jit(solution)/shard_map/ppermute | solution.py:15
  249.5 4.0 %collective-permute-start.15 = (bf16[128,1024]{1,0:T(8,128)(2,1)S(1)}, bf16[128,1024]{1,0:T(8,128)(2,1)S(1)}, u32[]{:S(2)}, u32[]{:S(2)}) collective-permute-start(bf16[128,1024]{1,0:T(8,128)(2,1)S(1)} %copy-done.4), channel_id=1, source_target_pairs={{0,1},{1,2},{2,3},{3,4},{4,5},{5,6},{6,7},{7,8},{8,9},{9,10},{10,1... | collective-permute-start | bytes 786440 | tf_op jit(solution)/shard_map/ppermute | solution.py:15
  253.5 9.5 %collective-permute-start.2 = (bf16[128,1024]{0,1:T(8,128)(2,1)S(1)}, bf16[128,1024]{0,1:T(8,128)(2,1)S(1)}, u32[]{:S(2)}, u32[]{:S(2)}) collective-permute-start(bf16[128,1024]{0,1:T(8,128)(2,1)S(1)} %copy.94), channel_id=1, source_target_pairs={{0,6},{1,7},{2,8},{3,9},{4,10},{5,11},{6,12},{7,13},{8,14},{9,15},... | collective-permute-start | bytes 786440 | tf_op jit(solution)/shard_map/ppermute | solution.py:15
  263.1 8.1 %collective-permute-start.3 = (bf16[128,1024]{0,1:T(8,128)(2,1)S(1)}, bf16[128,1024]{0,1:T(8,128)(2,1)S(1)}, u32[]{:S(2)}, u32[]{:S(2)}) collective-permute-start(bf16[128,1024]{0,1:T(8,128)(2,1)S(1)} %copy.94), channel_id=1, source_target_pairs={{0,5},{1,6},{2,7},{3,8},{4,9},{5,10},{6,11},{7,12},{8,13},{9,14},{... | collective-permute-start | bytes 786440 | tf_op jit(solution)/shard_map/ppermute | solution.py:15
  271.2 4.4 %collective-permute-start.4 = (bf16[128,1024]{0,1:T(8,128)(2,1)S(1)}, bf16[128,1024]{0,1:T(8,128)(2,1)S(1)}, u32[]{:S(2)}, u32[]{:S(2)}) collective-permute-start(bf16[128,1024]{0,1:T(8,128)(2,1)S(1)} %copy.94), channel_id=1, source_target_pairs={{0,4},{1,5},{2,6},{3,7},{4,8},{5,9},{6,10},{7,11},{8,12},{9,13},{1... | collective-permute-start | bytes 786440 | tf_op jit(solution)/shard_map/ppermute | solution.py:15
  275.6 4.6 %collective-permute-start.5 = (bf16[128,1024]{0,1:T(8,128)(2,1)S(1)}, bf16[128,1024]{0,1:T(8,128)(2,1)S(1)}, u32[]{:S(2)}, u32[]{:S(2)}) collective-permute-start(bf16[128,1024]{0,1:T(8,128)(2,1)S(1)} %copy.94), channel_id=1, source_target_pairs={{0,3},{1,4},{2,5},{3,6},{4,7},{5,8},{6,9},{7,10},{8,11},{9,12},{10... | collective-permute-start | bytes 786440 | tf_op jit(solution)/shard_map/ppermute | solution.py:15
  281.2 5.6 %collective-permute-start.6 = (bf16[128,1024]{0,1:T(8,128)(2,1)S(1)}, bf16[128,1024]{0,1:T(8,128)(2,1)}, u32[]{:S(2)}, u32[]{:S(2)}) collective-permute-start(bf16[128,1024]{0,1:T(8,128)(2,1)S(1)} %copy.94), channel_id=1, source_target_pairs={{0,2},{1,3},{2,4},{3,5},{4,6},{5,7},{6,8},{7,9},{8,10},{9,11},{10,... | collective-permute-start | bytes 786440 | tf_op jit(solution)/shard_map/ppermute | solution.py:15
  287.9 2.1 collective-permute-start.7
  290.2 12.9 %collective-permute-done.4 = bf16[128,1024]{0,1:T(8,128)(2,1)S(1)} collective-permute-done((bf16[128,1024]{0,1:T(8,128)(2,1)S(1)}, bf16[128,1024]{0,1:T(8,128)(2,1)S(1)}, u32[]{:S(2)}, u32[]{:S(2)}) %collective-permute-start.4) | collective-permute-done | bytes 262176 | tf_op jit(solution)/shard_map/ppermute | solution.py:15
  303.1 4.3 %copy.105 = bf16[1152,1024]{0,1:T(8,128)(2,1)} copy(bf16[1152,1024]{1,0:T(8,128)(2,1)} %copy-done) | data formatting | bytes 4718592 | tf_op jit(solution)/shard_map/concatenate | solution.py:111
  310.5 3.6 %fusion.51 = (f32[8,128]{1,0:T(8,128)S(1)}, bf16[8,128,1152]{1,2,0:T(8,128)(2,1)}) fusion(f32[8,1152,128]{2,1,0:T(8,128)S(1)} %convolution_multiply_fusion, pred[128,1152]{0,1:T(8,128)(4,1)S(1)} %fusion.43), kind=kOutput, calls=%fused_computation.75 | output fusion | flops 5899391 | bytes 7229440 | tf_op jit(solution)/shard_map/sub | solution.py:132
  314.2 4.6 %multiply_reduce_fusion = f32[8,128,128]{2,1,0:T(8,128)S(1)} fusion(bf16[8,16,128,128]{3,2,0,1:T(8,128)(2,1)} %all-to-all-done.2, f32[8,16,128]{2,0,1:T(8,128)S(1)} %get-tuple-element.120), kind=kLoop, calls=%fused_computation.21 | loop fusion | flops 6160384 | bytes 4784128 | tf_op jit(solution)/shard_map/reduce_sum | solution.py:69
  319.0 2.4 fusion.39
  (101 shorter events, 45.6 us)
Async XLA Ops:
  6.5 27.6 %copy-start.3 = (bf16[512,1024]{1,0:T(8,128)(2,1)S(1)}, bf16[512,1024]{1,0:T(8,128)(2,1)}, u32[]{:S(2)}) copy-start(bf16[512,1024]{1,0:T(8,128)(2,1)} %param.15) | copy-start | bytes 3145732
  6.5 91.1 %all-gather.2.cloned.1.call-start = ((), (), s32[]{:S(2)}) async-start(), calls=%async_computation.3 | async-start | bytes 4456448 | tf_op jit(solution)/shard_map/all_gather | solution.py:93
  9.6 266.1 %collective-permute-start = (bf16[128,1024]{0,1:T(8,128)(2,1)S(1)}, bf16[128,1024]{0,1:T(8,128)(2,1)}, u32[]{:S(2)}, u32[]{:S(2)}) collective-permute-start(bf16[128,1024]{0,1:T(8,128)(2,1)S(1)} %copy.94), channel_id=1, source_target_pairs={{0,8},{1,9},{2,10},{3,11},{4,12},{5,13},{6,14},{7,15},{8,16},{9,17... | collective-permute-start | bytes 786440 | tf_op jit(solution)/shard_map/ppermute | solution.py:15
  13.8 267.5 %collective-permute-start.1 = (bf16[128,1024]{0,1:T(8,128)(2,1)S(1)}, bf16[128,1024]{0,1:T(8,128)(2,1)}, u32[]{:S(2)}, u32[]{:S(2)}) collective-permute-start(bf16[128,1024]{0,1:T(8,128)(2,1)S(1)} %copy.94), channel_id=1, source_target_pairs={{0,7},{1,8},{2,9},{3,10},{4,11},{5,12},{6,13},{7,14},{8,15},{9,16}... | collective-permute-start | bytes 786440 | tf_op jit(solution)/shard_map/ppermute | solution.py:15
  17.2 171.3 %collective-permute-start.8 = (bf16[128,1024]{1,0:T(8,128)(2,1)}, bf16[128,1024]{1,0:T(8,128)(2,1)}, u32[]{:S(2)}, u32[]{:S(2)}) collective-permute-start(bf16[128,1024]{1,0:T(8,128)(2,1)} %param.13), channel_id=1, source_target_pairs={{0,8},{1,9},{2,10},{3,11},{4,12},{5,13},{6,14},{7,15},{8,16},{9,17... | collective-permute-start | bytes 786440 | tf_op jit(solution)/shard_map/ppermute | solution.py:15
  22.4 171.4 %collective-permute-start.9 = (bf16[128,1024]{1,0:T(8,128)(2,1)}, bf16[128,1024]{1,0:T(8,128)(2,1)}, u32[]{:S(2)}, u32[]{:S(2)}) collective-permute-start(bf16[128,1024]{1,0:T(8,128)(2,1)} %param.13), channel_id=1, source_target_pairs={{0,7},{1,8},{2,9},{3,10},{4,11},{5,12},{6,13},{7,14},{8,15},{9,16}... | collective-permute-start | bytes 786440 | tf_op jit(solution)/shard_map/ppermute | solution.py:15
  25.9 171.9 %collective-permute-start.10 = (bf16[128,1024]{1,0:T(8,128)(2,1)}, bf16[128,1024]{1,0:T(8,128)(2,1)}, u32[]{:S(2)}, u32[]{:S(2)}) collective-permute-start(bf16[128,1024]{1,0:T(8,128)(2,1)} %param.13), channel_id=1, source_target_pairs={{0,6},{1,7},{2,8},{3,9},{4,10},{5,11},{6,12},{7,13},{8,14},{9,15},... | collective-permute-start | bytes 786440 | tf_op jit(solution)/shard_map/ppermute | solution.py:15
  97.7 78.3 %copy-start.5 = (s32[4]{0:T(128)S(1)}, s32[4]{0:T(128)}, u32[]{:S(2)}) copy-start(s32[4]{0:T(128)} %param.18) | copy-start | bytes 52
  159.2 12.0 %all-to-all-start.1 = ((f32[8,16,128]{2,0,1:T(8,128)}), f32[8,16,128]{2,0,1:T(8,128)S(1)}, u32[]{:S(2)}, u32[]{:S(2)}) async-start(f32[8,16,128]{2,0,1:T(8,128)} %bitcast.7), calls=%async_computation.1 | async-start | bytes 131072 | tf_op jit(solution)/shard_map/all_to_all | solution.py:60
  171.2 11.1 %all-to-all-start = ((f32[8,16,128]{2,0,1:T(8,128)}), f32[8,16,128]{2,0,1:T(8,128)S(1)}, u32[]{:S(2)}, u32[]{:S(2)}) async-start(f32[8,16,128]{2,0,1:T(8,128)} %bitcast.6), calls=%async_computation | async-start | bytes 131072 | tf_op jit(solution)/shard_map/all_to_all | solution.py:61
  180.8 7.7 %copy-start.6 = (f32[8]{0:T(128)S(1)}, f32[8]{0:T(128)}, u32[]{:S(2)}) copy-start(f32[8]{0:T(128)} %param.19) | copy-start | bytes 100
  180.8 7.7 %copy-start.4 = (bf16[128,1024]{1,0:T(8,128)(2,1)S(1)}, bf16[128,1024]{1,0:T(8,128)(2,1)}, u32[]{:S(2)}) copy-start(bf16[128,1024]{1,0:T(8,128)(2,1)} %param.13) | copy-start | bytes 786436
  182.3 131.9 %all-to-all-start.2 = ((bf16[8,16,128,128]{3,2,0,1:T(8,128)(2,1)}), bf16[8,16,128,128]{3,2,0,1:T(8,128)(2,1)}, u32[]{:S(2)}, u32[]{:S(2)}) async-start(bf16[8,16,128,128]{3,2,0,1:T(8,128)(2,1)} %copy.91), calls=%async_computation.2 | async-start | bytes 8388608 | tf_op jit(solution)/shard_map/all_to_all | solution.py:56
  188.5 52.6 %collective-permute-start.11 = (bf16[128,1024]{1,0:T(8,128)(2,1)S(1)}, bf16[128,1024]{1,0:T(8,128)(2,1)S(1)}, u32[]{:S(2)}, u32[]{:S(2)}) collective-permute-start(bf16[128,1024]{1,0:T(8,128)(2,1)S(1)} %copy-done.4), channel_id=1, source_target_pairs={{0,5},{1,6},{2,7},{3,8},{4,9},{5,10},{6,11},{7,12},{8,13},{9,14},{... | collective-permute-start | bytes 786440 | tf_op jit(solution)/shard_map/ppermute | solution.py:15
  193.8 55.7 %collective-permute-start.12 = (bf16[128,1024]{1,0:T(8,128)(2,1)S(1)}, bf16[128,1024]{1,0:T(8,128)(2,1)S(1)}, u32[]{:S(2)}, u32[]{:S(2)}) collective-permute-start(bf16[128,1024]{1,0:T(8,128)(2,1)S(1)} %copy-done.4), channel_id=1, source_target_pairs={{0,4},{1,5},{2,6},{3,7},{4,8},{5,9},{6,10},{7,11},{8,12},{9,13},{1... | collective-permute-start | bytes 786440 | tf_op jit(solution)/shard_map/ppermute | solution.py:15
  197.9 55.7 %collective-permute-start.13 = (bf16[128,1024]{1,0:T(8,128)(2,1)S(1)}, bf16[128,1024]{1,0:T(8,128)(2,1)S(1)}, u32[]{:S(2)}, u32[]{:S(2)}) collective-permute-start(bf16[128,1024]{1,0:T(8,128)(2,1)S(1)} %copy-done.4), channel_id=1, source_target_pairs={{0,3},{1,4},{2,5},{3,6},{4,7},{5,8},{6,9},{7,10},{8,11},{9,12},{10... | collective-permute-start | bytes 786440 | tf_op jit(solution)/shard_map/ppermute | solution.py:15
  241.1 22.0 %collective-permute-start.14 = (bf16[128,1024]{1,0:T(8,128)(2,1)S(1)}, bf16[128,1024]{1,0:T(8,128)(2,1)S(1)}, u32[]{:S(2)}, u32[]{:S(2)}) collective-permute-start(bf16[128,1024]{1,0:T(8,128)(2,1)S(1)} %copy-done.4), channel_id=1, source_target_pairs={{0,2},{1,3},{2,4},{3,5},{4,6},{5,7},{6,8},{7,9},{8,10},{9,11},{10,... | collective-permute-start | bytes 786440 | tf_op jit(solution)/shard_map/ppermute | solution.py:15
  249.5 21.7 %collective-permute-start.15 = (bf16[128,1024]{1,0:T(8,128)(2,1)S(1)}, bf16[128,1024]{1,0:T(8,128)(2,1)S(1)}, u32[]{:S(2)}, u32[]{:S(2)}) collective-permute-start(bf16[128,1024]{1,0:T(8,128)(2,1)S(1)} %copy-done.4), channel_id=1, source_target_pairs={{0,1},{1,2},{2,3},{3,4},{4,5},{5,6},{6,7},{7,8},{8,9},{9,10},{10,1... | collective-permute-start | bytes 786440 | tf_op jit(solution)/shard_map/ppermute | solution.py:15
  253.5 34.3 %collective-permute-start.2 = (bf16[128,1024]{0,1:T(8,128)(2,1)S(1)}, bf16[128,1024]{0,1:T(8,128)(2,1)S(1)}, u32[]{:S(2)}, u32[]{:S(2)}) collective-permute-start(bf16[128,1024]{0,1:T(8,128)(2,1)S(1)} %copy.94), channel_id=1, source_target_pairs={{0,6},{1,7},{2,8},{3,9},{4,10},{5,11},{6,12},{7,13},{8,14},{9,15},... | collective-permute-start | bytes 786440 | tf_op jit(solution)/shard_map/ppermute | solution.py:15
  263.1 27.0 %collective-permute-start.3 = (bf16[128,1024]{0,1:T(8,128)(2,1)S(1)}, bf16[128,1024]{0,1:T(8,128)(2,1)S(1)}, u32[]{:S(2)}, u32[]{:S(2)}) collective-permute-start(bf16[128,1024]{0,1:T(8,128)(2,1)S(1)} %copy.94), channel_id=1, source_target_pairs={{0,5},{1,6},{2,7},{3,8},{4,9},{5,10},{6,11},{7,12},{8,13},{9,14},{... | collective-permute-start | bytes 786440 | tf_op jit(solution)/shard_map/ppermute | solution.py:15
  271.2 31.8 %collective-permute-start.4 = (bf16[128,1024]{0,1:T(8,128)(2,1)S(1)}, bf16[128,1024]{0,1:T(8,128)(2,1)S(1)}, u32[]{:S(2)}, u32[]{:S(2)}) collective-permute-start(bf16[128,1024]{0,1:T(8,128)(2,1)S(1)} %copy.94), channel_id=1, source_target_pairs={{0,4},{1,5},{2,6},{3,7},{4,8},{5,9},{6,10},{7,11},{8,12},{9,13},{1... | collective-permute-start | bytes 786440 | tf_op jit(solution)/shard_map/ppermute | solution.py:15
  275.6 14.5 %copy-start = (bf16[1152,1024]{1,0:T(8,128)(2,1)}, bf16[1152,1024]{1,0:T(8,128)(2,1)S(1)}, u32[]{:S(2)}) copy-start(bf16[1152,1024]{1,0:T(8,128)(2,1)S(1)} %constant_dynamic-update-slice_fusion) | copy-start | bytes 7077892
  275.6 31.8 %collective-permute-start.5 = (bf16[128,1024]{0,1:T(8,128)(2,1)S(1)}, bf16[128,1024]{0,1:T(8,128)(2,1)S(1)}, u32[]{:S(2)}, u32[]{:S(2)}) collective-permute-start(bf16[128,1024]{0,1:T(8,128)(2,1)S(1)} %copy.94), channel_id=1, source_target_pairs={{0,3},{1,4},{2,5},{3,6},{4,7},{5,8},{6,9},{7,10},{8,11},{9,12},{10... | collective-permute-start | bytes 786440 | tf_op jit(solution)/shard_map/ppermute | solution.py:15
  281.2 26.2 %collective-permute-start.6 = (bf16[128,1024]{0,1:T(8,128)(2,1)S(1)}, bf16[128,1024]{0,1:T(8,128)(2,1)}, u32[]{:S(2)}, u32[]{:S(2)}) collective-permute-start(bf16[128,1024]{0,1:T(8,128)(2,1)S(1)} %copy.94), channel_id=1, source_target_pairs={{0,2},{1,3},{2,4},{3,5},{4,6},{5,7},{6,8},{7,9},{8,10},{9,11},{10,... | collective-permute-start | bytes 786440 | tf_op jit(solution)/shard_map/ppermute | solution.py:15
  287.9 20.6 %collective-permute-start.7 = (bf16[128,1024]{0,1:T(8,128)(2,1)S(1)}, bf16[128,1024]{0,1:T(8,128)(2,1)}, u32[]{:S(2)}, u32[]{:S(2)}) collective-permute-start(bf16[128,1024]{0,1:T(8,128)(2,1)S(1)} %copy.94), channel_id=1, source_target_pairs={{0,1},{1,2},{2,3},{3,4},{4,5},{5,6},{6,7},{7,8},{8,9},{9,10},{10,1... | collective-permute-start | bytes 786440 | tf_op jit(solution)/shard_map/ppermute | solution.py:15
  303.1 6.5 %copy-start.2 = (bf16[128,1024]{1,0:T(8,128)(2,1)S(1)}, bf16[128,1024]{1,0:T(8,128)(2,1)}, u32[]{:S(2)}) copy-start(bf16[128,1024]{1,0:T(8,128)(2,1)} %param.11) | copy-start | bytes 786436
  314.2 4.8 %copy-start.1 = (bf16[1152,1024]{0,1:T(8,128)(2,1)S(1)}, bf16[1152,1024]{0,1:T(8,128)(2,1)}, u32[]{:S(2)}) copy-start(bf16[1152,1024]{0,1:T(8,128)(2,1)} %copy.105) | copy-start | bytes 7077892
Sparse Core Ops, SparseCore 0:
  10.3 87.2 all-gather.1
where the time goes:
time: 331 us; the launch traced here: 329 us
  waiting for transfers between devices  123 us (37%)
  starting transfers between devices  94.9 us (29%)
  local copies, waits for them, and re-layouts  46.5 us (14%)
  matrix products  32.1 us (10%)
  other arithmetic  18.8 us (6%)
  between operations  13.9 us (4%)
    ppermute x16, starting transfers between devices, from_behind(): return lax.ppermute(block, axis, route)  78.4 us
    all_gather x1, waiting for transfers between devices, on_device(): gathered = lax.all_gather(queries, 'mem', axis=0, tiled=True)  62.9 us
    ppermute x16, waiting for transfers between devices, from_behind(): return lax.ppermute(block, axis, route)  52 us
    dynamic_update_slice x16, local copies, waits for them, and re-layouts, owner_work(): return lax.map(owner_partial, (query_heads, key_heads, value_heads))  23.7 us
    dot_general x8, matrix products, owner_partial(): jnp.einsum('qd,kd->qk', query_head, key_head, preferred_element_type=jnp....  14.9 us
    dot_general x8, matrix products, owner_partial(): jnp.dot(weights.astype(jnp.bfloat16), value_head, preferred_element_type=...  13.8 us
    unnamed x34, local copies, waits for them, and re-layouts  12.4 us
    reduce_sum x8, other arithmetic, owner_partial(): totals = jnp.sum(weights, axis=1)  8.78 us
  transfers between devices with their start and end apart: 20, of which 5 were waited for; matrix products, arithmetic and copies ran while one was open for 27% of the time, Pallas kernels for 0%

commit v1 on v0

v1 whole, which is shorter than its diff:
```python
import functools

import jax
import jax.numpy as jnp
from jax import lax
from jax.experimental import pallas as pl
from jax.experimental.pallas import tpu as pltpu
from jax.sharding import PartitionSpec as P

MESH = pl.DeviceIdType.MESH

WINDOW = 1024
QBLK = 64
MBLK = 64
LIST = 8
HS = 128
HEADS = 8
MASKED = -1e30
LOG2E = 1.4426950408889634


def kernel(
    n_seq, n_mem, tok, shard,
    q_ref, k_ref, v_ref, mk_ref, mv_ref, slots_ref, docs_ref, gate_ref,
    out_ref,
    qbuf, kvbuf, membuf, lbuf, obuf,
    q_send, kv_send, q_recv, kv_recv, halo_send, halo_recv,
    mem_send, mem_recv, swap_send, swap_recv, out_send, out_recv,
):
    s = lax.axis_index("seq")
    m = lax.axis_index("mem")
    core = lax.rem(s, 2)
    head = m // 2
    parity = lax.rem(m, 2)
    nxt = lax.rem(s + 1, n_seq)
    prv = lax.rem(s + n_seq - 1, n_seq)
    partner = s + 1 - 2 * core
    n_rank = n_mem // 2
    blocks = shard // MBLK
    spare = n_rank * blocks
    group = n_mem * tok

    barrier = pltpu.get_barrier_semaphore()

    def greet(i, c):
        t = lax.rem(m + 1 + i, n_mem)
        pl.semaphore_signal(barrier, inc=1, device_id={"seq": s, "mem": t}, device_id_type=MESH)
        return c

    lax.fori_loop(0, n_mem - 1, greet, 0)
    for other in (nxt, prv):
        pl.semaphore_signal(barrier, inc=1, device_id={"seq": other, "mem": m}, device_id_type=MESH)

    def q_src(t):
        first = QBLK * lax.rem(lax.rem(t, 2) + m, 2)
        return q_ref.at[pl.ds(pl.multiple_of(first, QBLK), QBLK), pl.ds(pl.multiple_of((t // 2) * HS, HS), HS)]

    def kv_src(ref, t):
        return ref.at[:, pl.ds(pl.multiple_of((t // 2) * HS, HS), HS)]

    q_dst = qbuf.at[pl.ds(pl.multiple_of(m * QBLK, QBLK), QBLK)]
    kv_rows = pl.ds(pl.multiple_of(WINDOW + m * tok, tok), tok)
    mem_rows = pl.ds(head * blocks, blocks)

    pltpu.make_async_copy(q_src(m), q_dst, q_recv).start()
    pltpu.make_async_copy(kv_src(k_ref, m), kvbuf.at[0, kv_rows], kv_recv).start()
    pltpu.make_async_copy(kv_src(v_ref, m), kvbuf.at[1, kv_rows], kv_recv).start()

    def mem_src(ref, h):
        return ref.at[:, :, pl.ds(pl.multiple_of(h * HS, HS), HS)]

    mem_dst = membuf.at[core, mem_rows]

    @pl.when(core == 0)
    def _():
        pltpu.make_async_copy(mem_src(mk_ref, head), mem_dst, mem_recv.at[head]).start()

    @pl.when(core == 1)
    def _():
        pltpu.make_async_copy(mem_src(mv_ref, head), mem_dst, mem_recv.at[head]).start()

    membuf[:, spare] = jnp.zeros((2, MBLK, HS), jnp.bfloat16)
    pl.semaphore_wait(barrier, n_mem + 1)

    def send_qkv(i, c):
        t = lax.rem(m + 1 + i, n_mem)
        to = {"seq": s, "mem": t}
        pltpu.make_async_remote_copy(q_src(t), q_dst, q_send, q_recv, to, MESH).start()
        pltpu.make_async_remote_copy(kv_src(k_ref, t), kvbuf.at[0, kv_rows], kv_send, kv_recv, to, MESH).start()
        pltpu.make_async_remote_copy(kv_src(v_ref, t), kvbuf.at[1, kv_rows], kv_send, kv_recv, to, MESH).start()
        return c

    lax.fori_loop(0, n_mem - 1, send_qkv, 0)

    def send_mem(ref):
        def body(i, c):
            h = lax.rem(head + 1 + i, HEADS)
            to = {"seq": s, "mem": 2 * h + parity}
            pltpu.make_async_remote_copy(mem_src(ref, h), mem_dst, mem_send, mem_recv.at[head], to, MESH).start()
            return c

        lax.fori_loop(0, HEADS - 1, body, 0)

    @pl.when(core == 0)
    def _():
        send_mem(mk_ref)

    @pl.when(core == 1)
    def _():
        send_mem(mv_ref)

    def arrived(ref, sem):
        pltpu.make_async_copy(ref, ref, sem).wait()

    arrived(qbuf, q_recv)
    arrived(kvbuf.at[:, pl.ds(WINDOW, group)], kv_recv)
    halo = pltpu.make_async_remote_copy(
        kvbuf.at[:, pl.ds(group, WINDOW)], kvbuf.at[:, pl.ds(0, WINDOW)], halo_send, halo_recv,
        {"seq": nxt, "mem": m}, MESH,
    )
    halo.start()

    coef = float(HS) ** -0.5 * LOG2E
    keys = WINDOW + tok

    def half_of(b):
        return lax.rem(parity + b, 2)

    def local_block(b):
        q = qbuf[pl.ds(pl.multiple_of(b * QBLK, QBLK), QBLK), :]
        rows = pl.ds(pl.multiple_of(b * tok, tok), keys)
        sc = lax.dot_general(q, kvbuf[0, rows, :], (((1,), (1,)), ((), ())), preferred_element_type=jnp.float32)
        base = s * group + b * tok - WINDOW
        trel = WINDOW + QBLK * half_of(b) + lax.broadcasted_iota(jnp.int32, (QBLK, 1), 0)
        tpos = base + trel
        first = jnp.zeros((QBLK, 1), jnp.int32)
        for d in range(docs_ref.shape[0]):
            start = docs_ref[d]
            first = jnp.maximum(first, jnp.where(start <= tpos, start, 0))
        low = jnp.maximum(first - base, trel - (WINDOW - 1))
        col = lax.broadcasted_iota(jnp.int32, (QBLK, keys), 1)
        sc = jnp.where((col >= low) & (col <= trel), sc, MASKED)
        top = jnp.max(sc, axis=1, keepdims=True)
        w = jnp.exp2((sc - top) * coef)
        total = jnp.sum(w, axis=1, keepdims=True)
        acc = jnp.dot(w.astype(jnp.bfloat16), kvbuf[1, rows, :], preferred_element_type=jnp.float32)
        lbuf[pl.ds(pl.multiple_of(b * QBLK, QBLK), QBLK), :] = acc / total

    def local_range(lo, hi):
        def body(b, c):
            local_block(b)
            return c

        lax.fori_loop(lo, hi, body, 0)

    reach = WINDOW // tok
    local_range(reach, n_mem)

    def pass_on(r, c):
        piece = membuf.at[core, pl.ds(r * blocks, blocks)]
        arrived(piece, mem_recv.at[r])
        pltpu.make_async_remote_copy(piece, piece, swap_send, swap_recv, {"seq": partner, "mem": m}, MESH).start()
        return c

    lax.fori_loop(0, n_rank, pass_on, 0)

    halo.wait_recv()
    local_range(0, reach)

    arrived(membuf.at[1 - core, pl.ds(0, spare)], swap_recv)

    gate = jnp.full((1, HS), gate_ref[head], jnp.float32)
    gate = 1.0 / (1.0 + jnp.exp(-gate))
    lane_slot = lax.broadcasted_iota(jnp.int32, (1, LIST * MBLK), 1) // MBLK

    def out_copy(b):
        src = obuf.at[pl.ds(pl.multiple_of(b * QBLK, QBLK), QBLK)]
        return src

    out_rows_of = lambda b: pl.ds(pl.multiple_of(QBLK * half_of(b), QBLK), QBLK)
    out_cols = pl.ds(pl.multiple_of(head * HS, HS), HS)

    def mem_block(i, c):
        b = lax.rem(m + 1 + i, n_mem)
        row = 2 * b + half_of(b)
        place = jnp.zeros((1, LIST * MBLK), jnp.int32)
        for j in range(LIST):
            place = jnp.where(lane_slot == j, slots_ref[j, row], place)
        places = [slots_ref[j, row] for j in range(LIST)]
        q = qbuf[pl.ds(pl.multiple_of(b * QBLK, QBLK), QBLK), :]
        kk = jnp.concatenate([membuf[0, x] for x in places], axis=0)
        vv = jnp.concatenate([membuf[1, x] for x in places], axis=0)
        sc = lax.dot_general(q, kk, (((1,), (1,)), ((), ())), preferred_element_type=jnp.float32)
        sc = jnp.where(place < spare, sc, MASKED)
        top = jnp.max(sc, axis=1, keepdims=True)
        w = jnp.exp2((sc - top) * coef)
        total = jnp.sum(w, axis=1, keepdims=True)
        acc = jnp.dot(w.astype(jnp.bfloat16), vv, preferred_element_type=jnp.float32)
        rows = pl.ds(pl.multiple_of(b * QBLK, QBLK), QBLK)
        obuf[rows, :] = (gate * (acc / total) + (1.0 - gate) * lbuf[rows, :]).astype(jnp.bfloat16)
        dst = out_ref.at[out_rows_of(m), out_cols]

        @pl.when(b != m)
        def _():
            pltpu.make_async_remote_copy(
                obuf.at[rows], out_ref.at[out_rows_of(b), out_cols], out_send, out_recv,
                {"seq": s, "mem": b}, MESH,
            ).start()

        @pl.when(b == m)
        def _():
            pltpu.make_async_copy(obuf.at[rows], dst, out_recv).start()

        return c

    lax.fori_loop(0, n_mem, mem_block, 0)

    arrived(out_ref, out_recv)
    arrived(qbuf.at[pl.ds(0, (n_mem - 1) * QBLK)], q_send)
    arrived(kvbuf.at[:, pl.ds(0, (n_mem - 1) * tok)], kv_send)
    halo.wait_send()
    arrived(membuf.at[0, pl.ds(0, (HEADS - 1) * blocks)], mem_send)
    arrived(membuf.at[0, pl.ds(0, spare)], swap_send)
    arrived(obuf.at[pl.ds(0, (n_mem - 1) * QBLK)], out_send)


def list_slots(lists, counts, blocks, spare):
    lists = lists.T
    place = lists // (2 * blocks) * blocks + lists % blocks
    slot = jnp.arange(LIST, dtype=jnp.int32)
    earlier = (slot[None, :] < slot[:, None])[:, :, None]
    repeats = jnp.any((lists[:, None, :] == lists[None, :, :]) & earlier, axis=1)
    return jnp.where((slot[:, None] < counts[None, :]) & ~repeats, place, spare)


def solution(mesh):
    n_seq, n_mem = mesh.shape["seq"], mesh.shape["mem"]

    def on_device(q, k, v, mk, mv, lists, counts, docs, gate):
        tok, width = q.shape
        shard = mk.shape[0]
        group = n_mem * tok
        spare = n_mem // 2 * shard // MBLK
        by_block = lambda x: x.reshape(shard // MBLK, MBLK, width)
        hbm = pl.BlockSpec(memory_space=pl.ANY)
        smem = pl.BlockSpec(memory_space=pltpu.SMEM)
        dma = pltpu.SemaphoreType.DMA
        return pl.pallas_call(
            functools.partial(kernel, n_seq, n_mem, tok, shard),
            out_shape=jax.ShapeDtypeStruct((tok, width), jnp.bfloat16),
            in_specs=[hbm] * 5 + [smem] * 3,
            out_specs=hbm,
            scratch_shapes=[
                pltpu.VMEM((n_mem * QBLK, HS), jnp.bfloat16),
                pltpu.VMEM((2, WINDOW + group, HS), jnp.bfloat16),
                pltpu.VMEM((2, spare + 1, MBLK, HS), jnp.bfloat16),
                pltpu.VMEM((n_mem * QBLK, HS), jnp.float32),
                pltpu.VMEM((n_mem * QBLK, HS), jnp.bfloat16),
                dma, dma, dma, dma, dma, dma,
                dma, dma((n_mem // 2,)), dma, dma, dma, dma,
            ],
            compiler_params=pltpu.CompilerParams(
                collective_id=0, has_side_effects=True, vmem_limit_bytes=56 * 1024 * 1024
            ),
            name="memorizing_attention",
        )(q, k, v, by_block(mk), by_block(mv), list_slots(lists, counts, shard // MBLK, spare), docs, gate)

    in_specs = (
        P(("seq", "mem"), None),
        P(("seq", "mem"), None),
        P(("seq", "mem"), None),
        P("mem", None),
        P("mem", None),
        P("seq", None),
        P("seq"),
        P(),
        P(),
    )
    return jax.shard_map(
        on_device, mesh=mesh, in_specs=in_specs, out_specs=P(("seq", "mem"), None), check_vma=False
    )
```

time: 331 us -> 68.8 us (0.21)
  the two profiles are of different devices: /device:TPU:40 before, /device:TPU:2 now
where the time goes in v1:
time: 68.8 us; the launch traced here: 68.6 us
  Pallas kernels  64.9 us (94%)
  local copies, waits for them, and re-layouts  2.91 us (4%)
  other arithmetic  0.7 us (1%)
    pallas_call x1, Pallas kernels, on_device(): pl.pallas_call(functools.partial(kernel, n_seq, n_mem, tok, shard), out_s...  64.9 us
    unnamed x5, local copies, waits for them, and re-layouts  2.91 us

profile of v1, /device:TPU:2, one launch (start us, length us, event | category | flops | bytes accessed | tf_op | source)
XLA Modules:
  0.0 68.6 jit_solution(10812410851322158001)
XLA Ops:
  0.0 0.0 copy-start
  0.0 0.7 copy-done
  0.7 0.0 copy-start.1
  0.7 0.1 and_reduce_fusion
  0.8 0.6 copy-done.1
  1.3 0.6 fusion.3.slots_ref
  1.9 64.9 %memorizing_attention.1 = bf16[128,1024]{1,0:T(8,128)(2,1)} custom-call(bf16[128,1024]{1,0:T(8,128)(2,1)} %q_ref.1, bf16[128,1024]{1,0:T(8,128)(2,1)} %k_ref.1, bf16[128,1024]{1,0:T(8,128)(2,1)} %v_ref.1, bf16[8,64,1024]{2,1,0:T(8,128)(2,1)} %bitcast.4, bf16[8,64,1024]{2,1,0:T(8,128)(2,1)} %bitcast.5, s32[8,32]{1,0:T(8,128)} %fusion.3.slots_ref, s32[4]{0:T(128)} %docs_ref.1, ...), custom_call_target="tpu_custom_call" | custom-call | tf_op jit(solution)/shard_map/memorizing_attention/pallas_call | solution.py:248
  66.9 1.7 %copy.11 = bf16[128,1024]{1,0:T(8,128)(2,1)} copy(bf16[128,1024]{1,0:T(8,128)(2,1)} %memorizing_attention.1) | data formatting | bytes 524288
  (1 shorter events, 0.0 us)
Async XLA Ops:
  0.0 0.7 %copy-start = (s32[32,8]{0,1:T(8,128)S(1)}, s32[32,8]{0,1:T(8,128)}, u32[]{:S(2)}) copy-start(s32[32,8]{0,1:T(8,128)} %param.14) | copy-start | bytes 3076
  0.7 0.7 copy-start.1

commit v2 on v1

v2 whole, which is shorter than its diff:
```python
import functools

import jax
import jax.numpy as jnp
from jax import lax
from jax.experimental import pallas as pl
from jax.experimental.pallas import tpu as pltpu
from jax.sharding import PartitionSpec as P

MESH = pl.DeviceIdType.MESH

WINDOW = 1024
QBLK = 64
MBLK = 64
LIST = 8
HS = 128
HEADS = 8
BATCH = 4
MASKED = -1e30
LOG2E = 1.4426950408889634
COEF = float(HS) ** -0.5 * LOG2E


def aligned(first, size):
    return pl.ds(pl.multiple_of(first, size), size)


def arrived(ref, sem):
    pltpu.make_async_copy(ref, ref, sem).wait()


def kernel(
    n_seq, n_mem, tok, shard,
    q_ref, k_ref, v_ref, mk_ref, mv_ref, lists_ref, counts_ref, docs_ref, gate_ref,
    out_ref,
    qbuf, kvbuf, membuf, mixed, obuf, lists, counts, slots_vmem, slots, docs, gates,
    small_sem, slot_sem, q_send, kv_send, q_recv, kv_recv, halo_send, halo_recv,
    mem_send, mem_recv, z_send, z_recv, swap_send, swap_recv, out_send, out_recv,
):
    s = lax.axis_index("seq")
    m = lax.axis_index("mem")
    core = lax.rem(s, 2)
    z_half = lax.rem(s // 2, 2)
    head = m // 2
    parity = lax.rem(m, 2)
    nxt = {"seq": lax.rem(s + 1, n_seq), "mem": m}
    prv = {"seq": lax.rem(s + n_seq - 1, n_seq), "mem": m}
    up = {"seq": lax.rem(s + 2, n_seq), "mem": m}
    down = {"seq": lax.rem(s + n_seq - 2, n_seq), "mem": m}
    along_z = {"seq": lax.rem(s + 2 - 4 * core + n_seq, n_seq), "mem": m}
    partner = {"seq": s + 1 - 2 * core, "mem": m}
    n_rank = n_mem // 2
    blocks = shard // MBLK
    half = blocks // 2
    spare = n_rank * blocks
    group = n_mem * tok

    smalls = (
        pltpu.make_async_copy(lists_ref, lists, small_sem.at[0]),
        pltpu.make_async_copy(counts_ref, counts, small_sem.at[1]),
        pltpu.make_async_copy(docs_ref, docs, small_sem.at[2]),
        pltpu.make_async_copy(gate_ref, gates, small_sem.at[3]),
    )
    for copy in smalls:
        copy.start()

    barrier = pltpu.get_barrier_semaphore()

    def greet(i, c):
        t = lax.rem(m + 1 + i, n_mem)
        pl.semaphore_signal(barrier, inc=1, device_id={"seq": s, "mem": t}, device_id_type=MESH)
        return c

    lax.fori_loop(0, n_mem - 1, greet, 0)
    for other in (nxt, prv, up, down):
        pl.semaphore_signal(barrier, inc=1, device_id=other, device_id_type=MESH)

    def cols(h):
        return aligned(h * HS, HS)

    def q_src(t):
        first = QBLK * lax.rem(lax.rem(t, 2) + m, 2)
        return q_ref.at[aligned(first, QBLK), cols(t // 2)]

    def kv_src(ref, t):
        return ref.at[:, cols(t // 2)]

    def mem_src(ref, h):
        return ref.at[pl.ds(z_half * half, half), :, cols(h)]

    def piece(r, z):
        return membuf.at[core, pl.ds(r * blocks + z * half, half)]

    def kv_rows(src):
        return aligned(WINDOW + src * tok, tok)

    q_dst = qbuf.at[aligned(m * QBLK, QBLK)]
    mem_dst = piece(head, z_half)
    for on_core, ref in ((0, mk_ref), (1, mv_ref)):

        @pl.when(core == on_core)
        def _(ref=ref):
            pltpu.make_async_copy(mem_src(ref, head), mem_dst, mem_recv.at[head]).start()

    pltpu.make_async_copy(q_src(m), q_dst, q_recv).start()
    for kind, ref in enumerate((k_ref, v_ref)):
        pltpu.make_async_copy(kv_src(ref, m), kvbuf.at[kind, kv_rows(m)], kv_recv.at[m]).start()

    membuf[:, spare] = jnp.zeros((2, MBLK, HS), jnp.bfloat16)
    pl.semaphore_wait(barrier, n_mem + 3)

    for on_core, ref in ((0, mk_ref), (1, mv_ref)):

        @pl.when(core == on_core)
        def _(ref=ref):
            def body(i, c):
                h = lax.rem(head + 1 + i, HEADS)
                to = {"seq": s, "mem": 2 * h + parity}
                pltpu.make_async_remote_copy(
                    mem_src(ref, h), mem_dst, mem_send, mem_recv.at[head], to, MESH
                ).start()
                return c

            lax.fori_loop(0, HEADS - 1, body, 0)

    def send_q(i, c):
        t = lax.rem(m + 1 + i, n_mem)
        to = {"seq": s, "mem": t}
        pltpu.make_async_remote_copy(q_src(t), q_dst, q_send, q_recv, to, MESH).start()
        return c

    lax.fori_loop(0, n_mem - 1, send_q, 0)

    def send_kv(i, c):
        t = lax.rem(m + 1 + i, n_mem)
        to = {"seq": s, "mem": t}
        for kind, ref in enumerate((k_ref, v_ref)):
            pltpu.make_async_remote_copy(
                kv_src(ref, t), kvbuf.at[kind, kv_rows(m)], kv_send, kv_recv.at[m], to, MESH
            ).start()
        return c

    lax.fori_loop(0, n_mem - 1, send_kv, 0)

    for copy in smalls:
        copy.wait()
    named = [lists[j : j + 1, :] for j in range(LIST)]
    for j in range(LIST):
        ok = j < counts[...]
        for e in range(j):
            ok = ok & (named[e] != named[j])
        place = lax.shift_right_logical(named[j], 4) * blocks + (named[j] & (blocks - 1))
        slots_vmem[j : j + 1, :] = jnp.where(ok, place, spare)
    to_slots = pltpu.make_async_copy(slots_vmem, slots, slot_sem)
    to_slots.start()

    def pass_first(i, c):
        r = lax.rem(head + n_rank - i, n_rank)
        got = piece(r, z_half)
        arrived(got, mem_recv.at[r])
        pltpu.make_async_remote_copy(got, got, z_send, z_recv.at[r], along_z, MESH).start()
        pltpu.make_async_remote_copy(got, got, swap_send, swap_recv, partner, MESH).start()
        return c

    lax.fori_loop(0, n_rank, pass_first, 0)

    def pass_second(i, c):
        r = lax.rem(head + n_rank - i, n_rank)
        got = piece(r, 1 - z_half)
        arrived(got, z_recv.at[r])
        pltpu.make_async_remote_copy(got, got, swap_send, swap_recv, partner, MESH).start()
        return c

    lax.fori_loop(0, n_rank, pass_second, 0)

    to_slots.wait()
    arrived(qbuf, q_recv)
    arrived(membuf.at[1 - core, pl.ds(0, spare)], swap_recv)

    gate = 1.0 / (1.0 + jnp.exp(-jnp.full((1, HS), gates[head], jnp.float32)))
    lane_slot = lax.broadcasted_iota(jnp.int32, (1, LIST * MBLK), 1) // MBLK

    def half_of(b):
        return lax.rem(parity + b, 2)

    def softmax(sc):
        w = jnp.exp2((sc - jnp.max(sc, axis=1, keepdims=True)) * COEF)
        return w.astype(jnp.bfloat16), jnp.sum(w, axis=1, keepdims=True)

    def scores(q, k):
        return lax.dot_general(q, k, (((1,), (1,)), ((), ())), preferred_element_type=jnp.float32)

    def mem_block(b, c):
        row = 2 * b + half_of(b)
        place = jnp.zeros((1, LIST * MBLK), jnp.int32)
        for j in range(LIST):
            place = jnp.where(lane_slot == j, slots[j, row], place)
        places = [slots[j, row] for j in range(LIST)]
        rows = aligned(b * QBLK, QBLK)
        kk = jnp.concatenate([membuf[0, x] for x in places], axis=0)
        vv = jnp.concatenate([membuf[1, x] for x in places], axis=0)
        w, total = softmax(jnp.where(place < spare, scores(qbuf[rows, :], kk), MASKED))
        mixed[rows, :] = gate * (jnp.dot(w, vv, preferred_element_type=jnp.float32) / total)
        return c

    lax.fori_loop(0, n_mem, mem_block, 0, unroll=2)

    reach = WINDOW // tok

    def pass_halo(i, c):
        src = lax.rem(m + n_mem - i, n_mem)
        arrived(kvbuf.at[:, kv_rows(src)], kv_recv.at[src])

        @pl.when(src >= n_mem - reach)
        def _():
            dst = kvbuf.at[:, aligned((src - (n_mem - reach)) * tok, tok)]
            pltpu.make_async_remote_copy(
                kvbuf.at[:, kv_rows(src)], dst, halo_send, halo_recv, nxt, MESH
            ).start()

        return c

    lax.fori_loop(0, n_mem, pass_halo, 0)

    keys = WINDOW + BATCH * tok
    batches = n_mem // BATCH

    def local_batch(i, c):
        b = BATCH * i
        rows = aligned(b * QBLK, BATCH * QBLK)
        span = pl.ds(pl.multiple_of(b * tok, tok), keys)
        sc = scores(qbuf[rows, :], kvbuf[0, span, :])
        row = lax.broadcasted_iota(jnp.int32, (BATCH * QBLK, 1), 0)
        block = row // QBLK
        until = WINDOW + block * tok + QBLK * lax.rem(parity + block, 2) + lax.rem(row, QBLK)
        base = s * group + b * tok - WINDOW
        token = base + until
        first = jnp.zeros((BATCH * QBLK, 1), jnp.int32)
        for d in range(docs_ref.shape[0]):
            start = docs[d]
            first = jnp.maximum(first, jnp.where(start <= token, start, 0))
        low = jnp.maximum(first - base, until - (WINDOW - 1))
        col = lax.broadcasted_iota(jnp.int32, (BATCH * QBLK, keys), 1)
        sc = jnp.where(col >= low, sc, MASKED)
        tail = jnp.where(col[:, WINDOW:] <= until, sc[:, WINDOW:], MASKED)
        w, total = softmax(jnp.concatenate([sc[:, :WINDOW], tail], axis=1))
        local = jnp.dot(w, kvbuf[1, span, :], preferred_element_type=jnp.float32) / total
        obuf[rows, :] = (mixed[rows, :] + (1.0 - gate) * local).astype(jnp.bfloat16)
        for j in range(BATCH):
            t = b + j
            src = obuf.at[aligned(t * QBLK, QBLK)]
            dst = out_ref.at[aligned(QBLK * half_of(t), QBLK), cols(head)]

            @pl.when(t != m)
            def _():
                pltpu.make_async_remote_copy(
                    src, dst, out_send, out_recv, {"seq": s, "mem": t}, MESH
                ).start()

            @pl.when(t == m)
            def _():
                pltpu.make_async_copy(src, dst, out_recv).start()

        return c

    lax.fori_loop(batches // 2, batches, local_batch, 0)
    arrived(kvbuf.at[:, pl.ds(0, WINDOW)], halo_recv)
    lax.fori_loop(0, batches // 2, local_batch, 0)

    arrived(mem_dst_all(membuf, 0, (HEADS - 1) * half), mem_send)
    arrived(mem_dst_all(membuf, 0, n_rank * half), z_send)
    arrived(mem_dst_all(membuf, 0, spare), swap_send)
    arrived(qbuf.at[pl.ds(0, (n_mem - 1) * QBLK)], q_send)
    arrived(kvbuf.at[:, pl.ds(0, (n_mem - 1) * tok)], kv_send)
    arrived(kvbuf.at[:, pl.ds(0, WINDOW)], halo_send)
    arrived(obuf.at[pl.ds(0, (n_mem - 1) * QBLK)], out_send)
    arrived(out_ref, out_recv)


def mem_dst_all(membuf, kind, count):
    return membuf.at[kind, pl.ds(0, count)]


def solution(mesh):
    n_seq, n_mem = mesh.shape["seq"], mesh.shape["mem"]

    def on_device(q, k, v, mk, mv, lists, counts, docs, gate):
        tok, width = q.shape
        shard = mk.shape[0]
        group = n_mem * tok
        spare = n_mem // 2 * shard // MBLK
        lists = lists.T
        counts = counts.reshape(1, -1)
        by_block = lambda x: x.reshape(shard // MBLK, MBLK, width)
        hbm = pl.BlockSpec(memory_space=pl.ANY)
        dma = pltpu.SemaphoreType.DMA
        return pl.pallas_call(
            functools.partial(kernel, n_seq, n_mem, tok, shard),
            out_shape=jax.ShapeDtypeStruct((tok, width), jnp.bfloat16),
            in_specs=[hbm] * 9,
            out_specs=hbm,
            scratch_shapes=[
                pltpu.VMEM((n_mem * QBLK, HS), jnp.bfloat16),
                pltpu.VMEM((2, WINDOW + group, HS), jnp.bfloat16),
                pltpu.VMEM((2, spare + 1, MBLK, HS), jnp.bfloat16),
                pltpu.VMEM((n_mem * QBLK, HS), jnp.float32),
                pltpu.VMEM((n_mem * QBLK, HS), jnp.bfloat16),
                pltpu.VMEM(lists.shape, jnp.int32),
                pltpu.VMEM(counts.shape, jnp.int32),
                pltpu.VMEM(lists.shape, jnp.int32),
                pltpu.SMEM(lists.shape, jnp.int32),
                pltpu.SMEM(docs.shape, jnp.int32),
                pltpu.SMEM(gate.shape, jnp.float32),
                dma((4,)), dma, dma, dma, dma, dma((n_mem,)), dma, dma,
                dma, dma((n_mem // 2,)), dma, dma((n_mem // 2,)), dma, dma, dma, dma,
            ],
            compiler_params=pltpu.CompilerParams(
                collective_id=0, has_side_effects=True, vmem_limit_bytes=56 * 1024 * 1024
            ),
            name="memorizing_attention",
        )(q, k, v, by_block(mk), by_block(mv), lists, counts, docs, gate)

    in_specs = (
        P(("seq", "mem"), None),
        P(("seq", "mem"), None),
        P(("seq", "mem"), None),
        P("mem", None),
        P("mem", None),
        P("seq", None),
        P("seq"),
        P(),
        P(),
    )
    return jax.shard_map(
        on_device, mesh=mesh, in_specs=in_specs, out_specs=P(("seq", "mem"), None), check_vma=False
    )
```

time: 68.8 us -> 53.3 us (0.77)
  the two profiles are of different devices: /device:TPU:2 before, /device:TPU:6 now
where the time goes in v2:
time: 53.3 us; the launch traced here: 53.2 us
  Pallas kernels  51.5 us (97%)
  local copies, waits for them, and re-layouts  1.67 us (3%)
    pallas_call x1, Pallas kernels, on_device(): pl.pallas_call(functools.partial(kernel, n_seq, n_mem, tok, shard), out_s...  51.5 us
    unnamed x1, local copies, waits for them, and re-layouts  1.67 us

profile of v2, /device:TPU:6, one launch (start us, length us, event | category | flops | bytes accessed | tf_op | source)
XLA Modules:
  0.0 53.2 jit_solution(15266434923299852759)
XLA Ops:
  0.0 51.5 %memorizing_attention.1 = bf16[128,1024]{1,0:T(8,128)(2,1)} custom-call(bf16[128,1024]{1,0:T(8,128)(2,1)} %q_ref.1, bf16[128,1024]{1,0:T(8,128)(2,1)} %k_ref.1, bf16[128,1024]{1,0:T(8,128)(2,1)} %v_ref.1, bf16[8,64,1024]{2,1,0:T(8,128)(2,1)} %bitcast.4, bf16[8,64,1024]{2,1,0:T(8,128)(2,1)} %bitcast.5, s32[8,32]{1,0:T(8,128)} %bitcast.6, s32[1,32]{1,0:T(1,128)} %bitcast.7, ...), custom_call_target="tpu_custom_call" | custom-call | tf_op jit(solution)/shard_map/memorizing_attention/pallas_call | solution.py:297
  51.5 1.7 %copy.11 = bf16[128,1024]{1,0:T(8,128)(2,1)} copy(bf16[128,1024]{1,0:T(8,128)(2,1)} %memorizing_attention.1) | data formatting | bytes 524288

commit v3 on v2

--- a/solution.py
+++ b/solution.py
@@ -43,11 +43,10 @@
     z_half = lax.rem(s // 2, 2)
     head = m // 2
     parity = lax.rem(m, 2)
-    nxt = {"seq": lax.rem(s + 1, n_seq), "mem": m}
-    prv = {"seq": lax.rem(s + n_seq - 1, n_seq), "mem": m}
-    up = {"seq": lax.rem(s + 2, n_seq), "mem": m}
-    down = {"seq": lax.rem(s + n_seq - 2, n_seq), "mem": m}
-    along_z = {"seq": lax.rem(s + 2 - 4 * core + n_seq, n_seq), "mem": m}
+    has_prv, has_nxt = s > 0, s < n_seq - 1
+    nxt = {"seq": s + 1, "mem": m}
+    prv = {"seq": s - 1, "mem": m}
+    along_z = {"seq": s + 2 - 4 * z_half, "mem": m}
     partner = {"seq": s + 1 - 2 * core, "mem": m}
     n_rank = n_mem // 2
     blocks = shard // MBLK
@@ -72,8 +71,11 @@
         return c
 
     lax.fori_loop(0, n_mem - 1, greet, 0)
-    for other in (nxt, prv, up, down):
-        pl.semaphore_signal(barrier, inc=1, device_id=other, device_id_type=MESH)
+    for there, other in ((has_nxt, nxt), (has_prv, prv), (s >= 0, along_z)):
+
+        @pl.when(there)
+        def _(other=other):
+            pl.semaphore_signal(barrier, inc=1, device_id=other, device_id_type=MESH)
 
     def cols(h):
         return aligned(h * HS, HS)
@@ -107,7 +109,20 @@
         pltpu.make_async_copy(kv_src(ref, m), kvbuf.at[kind, kv_rows(m)], kv_recv.at[m]).start()
 
     membuf[:, spare] = jnp.zeros((2, MBLK, HS), jnp.bfloat16)
-    pl.semaphore_wait(barrier, n_mem + 3)
+
+    @pl.when(jnp.logical_not(has_prv))
+    def _():
+        kvbuf[:, :WINDOW] = jnp.zeros((2, WINDOW, HS), jnp.bfloat16)
+
+    inner = has_prv & has_nxt
+
+    @pl.when(inner)
+    def _():
+        pl.semaphore_wait(barrier, n_mem + 2)
+
+    @pl.when(jnp.logical_not(inner))
+    def _():
+        pl.semaphore_wait(barrier, n_mem + 1)
 
     for on_core, ref in ((0, mk_ref), (1, mv_ref)):
 
@@ -173,10 +188,6 @@
 
     lax.fori_loop(0, n_rank, pass_second, 0)
 
-    to_slots.wait()
-    arrived(qbuf, q_recv)
-    arrived(membuf.at[1 - core, pl.ds(0, spare)], swap_recv)
-
     gate = 1.0 / (1.0 + jnp.exp(-jnp.full((1, HS), gates[head], jnp.float32)))
     lane_slot = lax.broadcasted_iota(jnp.int32, (1, LIST * MBLK), 1) // MBLK
 
@@ -203,24 +214,39 @@
         mixed[rows, :] = gate * (jnp.dot(w, vv, preferred_element_type=jnp.float32) / total)
         return c
 
-    lax.fori_loop(0, n_mem, mem_block, 0, unroll=2)
 
     reach = WINDOW // tok
 
+    late = n_mem - reach
+
+    def take(src):
+        arrived(kvbuf.at[:, kv_rows(src)], kv_recv.at[src])
+
     def pass_halo(i, c):
-        src = lax.rem(m + n_mem - i, n_mem)
-        arrived(kvbuf.at[:, kv_rows(src)], kv_recv.at[src])
-
-        @pl.when(src >= n_mem - reach)
+        place = lax.rem(m + n_mem - i, reach)
+        src = late + place
+        take(src)
+
+        @pl.when(has_nxt)
         def _():
-            dst = kvbuf.at[:, aligned((src - (n_mem - reach)) * tok, tok)]
+            dst = kvbuf.at[:, aligned(place * tok, tok)]
             pltpu.make_async_remote_copy(
                 kvbuf.at[:, kv_rows(src)], dst, halo_send, halo_recv, nxt, MESH
             ).start()
 
         return c
 
-    lax.fori_loop(0, n_mem, pass_halo, 0)
+    lax.fori_loop(0, reach, pass_halo, 0)
+    to_slots.wait()
+    arrived(qbuf, q_recv)
+    arrived(membuf.at[1 - core, pl.ds(0, spare)], swap_recv)
+    lax.fori_loop(0, n_mem, mem_block, 0, unroll=2)
+
+    def take_rest(src, c):
+        take(src)
+        return c
+
+    lax.fori_loop(0, late, take_rest, 0)
 
     keys = WINDOW + BATCH * tok
     batches = n_mem // BATCH
@@ -264,7 +290,11 @@
         return c
 
     lax.fori_loop(batches // 2, batches, local_batch, 0)
-    arrived(kvbuf.at[:, pl.ds(0, WINDOW)], halo_recv)
+
+    @pl.when(has_prv)
+    def _():
+        arrived(kvbuf.at[:, pl.ds(0, WINDOW)], halo_recv)
+
     lax.fori_loop(0, batches // 2, local_batch, 0)
 
     arrived(mem_dst_all(membuf, 0, (HEADS - 1) * half), mem_send)
@@ -272,7 +302,11 @@
     arrived(mem_dst_all(membuf, 0, spare), swap_send)
     arrived(qbuf.at[pl.ds(0, (n_mem - 1) * QBLK)], q_send)
     arrived(kvbuf.at[:, pl.ds(0, (n_mem - 1) * tok)], kv_send)
-    arrived(kvbuf.at[:, pl.ds(0, WINDOW)], halo_send)
+
+    @pl.when(has_nxt)
+    def _():
+        arrived(kvbuf.at[:, pl.ds(0, WINDOW)], halo_send)
+
     arrived(obuf.at[pl.ds(0, (n_mem - 1) * QBLK)], out_send)
     arrived(out_ref, out_recv)
 

time: 53.3 us -> 47.4 us (0.89)
  the two profiles are of different devices: /device:TPU:6 before, /device:TPU:37 now
where the time goes in v3:
time: 47.4 us; the launch traced here: 47.3 us
  Pallas kernels  45.6 us (96%)
  local copies, waits for them, and re-layouts  1.67 us (4%)
    pallas_call x1, Pallas kernels, on_device(): pl.pallas_call(functools.partial(kernel, n_seq, n_mem, tok, shard), out_s...  45.6 us
    unnamed x1, local copies, waits for them, and re-layouts  1.67 us

profile of v3, /device:TPU:37, one launch (start us, length us, event | category | flops | bytes accessed | tf_op | source)
XLA Modules:
  0.0 47.3 jit_solution(789681957296243138)
XLA Ops:
  0.0 45.6 %memorizing_attention.1 = bf16[128,1024]{1,0:T(8,128)(2,1)} custom-call(bf16[128,1024]{1,0:T(8,128)(2,1)} %q_ref.1, bf16[128,1024]{1,0:T(8,128)(2,1)} %k_ref.1, bf16[128,1024]{1,0:T(8,128)(2,1)} %v_ref.1, bf16[8,64,1024]{2,1,0:T(8,128)(2,1)} %bitcast.4, bf16[8,64,1024]{2,1,0:T(8,128)(2,1)} %bitcast.5, s32[8,32]{1,0:T(8,128)} %bitcast.6, s32[1,32]{1,0:T(1,128)} %bitcast.7, ...), custom_call_target="tpu_custom_call" | custom-call | tf_op jit(solution)/shard_map/memorizing_attention/pallas_call | solution.py:331
  45.6 1.7 %copy.11 = bf16[128,1024]{1,0:T(8,128)(2,1)} copy(bf16[128,1024]{1,0:T(8,128)(2,1)} %memorizing_attention.1) | data formatting | bytes 524288

commit v4 on v3

--- a/solution.py
+++ b/solution.py
@@ -16,6 +16,7 @@
 HS = 128
 HEADS = 8
 BATCH = 4
+OWN = 4
 MASKED = -1e30
 LOG2E = 1.4426950408889634
 COEF = float(HS) ** -0.5 * LOG2E
@@ -50,7 +51,7 @@
     partner = {"seq": s + 1 - 2 * core, "mem": m}
     n_rank = n_mem // 2
     blocks = shard // MBLK
-    half = blocks // 2
+    swapped = blocks - OWN
     spare = n_rank * blocks
     group = n_mem * tok
 
@@ -88,16 +89,19 @@
         return ref.at[:, cols(t // 2)]
 
     def mem_src(ref, h):
-        return ref.at[pl.ds(z_half * half, half), :, cols(h)]
-
-    def piece(r, z):
-        return membuf.at[core, pl.ds(r * blocks + z * half, half)]
+        return ref.at[pl.ds(z_half * swapped, OWN), :, cols(h)]
+
+    def fetched(r):
+        return membuf.at[core, pl.ds(r * blocks + z_half * swapped, OWN)]
+
+    def along(r, z):
+        return membuf.at[core, pl.ds(r * blocks + z * OWN, swapped)]
 
     def kv_rows(src):
         return aligned(WINDOW + src * tok, tok)
 
     q_dst = qbuf.at[aligned(m * QBLK, QBLK)]
-    mem_dst = piece(head, z_half)
+    mem_dst = fetched(head)
     for on_core, ref in ((0, mk_ref), (1, mv_ref)):
 
         @pl.when(core == on_core)
@@ -155,7 +159,6 @@
             ).start()
         return c
 
-    lax.fori_loop(0, n_mem - 1, send_kv, 0)
 
     for copy in smalls:
         copy.wait()
@@ -171,17 +174,18 @@
 
     def pass_first(i, c):
         r = lax.rem(head + n_rank - i, n_rank)
-        got = piece(r, z_half)
+        got, gives = fetched(r), along(r, z_half)
         arrived(got, mem_recv.at[r])
-        pltpu.make_async_remote_copy(got, got, z_send, z_recv.at[r], along_z, MESH).start()
+        pltpu.make_async_remote_copy(gives, gives, z_send, z_recv.at[r], along_z, MESH).start()
         pltpu.make_async_remote_copy(got, got, swap_send, swap_recv, partner, MESH).start()
         return c
 
     lax.fori_loop(0, n_rank, pass_first, 0)
+    lax.fori_loop(0, n_mem - 1, send_kv, 0)
 
     def pass_second(i, c):
         r = lax.rem(head + n_rank - i, n_rank)
-        got = piece(r, 1 - z_half)
+        got = along(r, 1 - z_half)
         arrived(got, z_recv.at[r])
         pltpu.make_async_remote_copy(got, got, swap_send, swap_recv, partner, MESH).start()
         return c
@@ -201,19 +205,29 @@
     def scores(q, k):
         return lax.dot_general(q, k, (((1,), (1,)), ((), ())), preferred_element_type=jnp.float32)
 
-    def mem_block(b, c):
-        row = 2 * b + half_of(b)
-        place = jnp.zeros((1, LIST * MBLK), jnp.int32)
-        for j in range(LIST):
-            place = jnp.where(lane_slot == j, slots[j, row], place)
-        places = [slots[j, row] for j in range(LIST)]
-        rows = aligned(b * QBLK, QBLK)
-        kk = jnp.concatenate([membuf[0, x] for x in places], axis=0)
-        vv = jnp.concatenate([membuf[1, x] for x in places], axis=0)
-        w, total = softmax(jnp.where(place < spare, scores(qbuf[rows, :], kk), MASKED))
-        mixed[rows, :] = gate * (jnp.dot(w, vv, preferred_element_type=jnp.float32) / total)
-        return c
-
+    def mem_pair(i, c):
+        keys, values, places = [], [], []
+        for b in (2 * i, 2 * i + 1):
+            row = 2 * b + half_of(b)
+            ids = [slots[j, row] for j in range(LIST)]
+            place = jnp.zeros((1, LIST * MBLK), jnp.int32)
+            for j in range(LIST):
+                place = jnp.where(lane_slot == j, ids[j], place)
+            keys.append(jnp.concatenate([membuf[0, x] for x in ids], axis=0))
+            values.append(jnp.concatenate([membuf[1, x] for x in ids], axis=0))
+            places.append(jnp.broadcast_to(place, (QBLK, LIST * MBLK)))
+        rows = aligned(2 * i * QBLK, 2 * QBLK)
+        q = qbuf[rows, :]
+        none = jnp.zeros((QBLK, HS), jnp.bfloat16)
+        q = jnp.concatenate(
+            [jnp.concatenate([q[:QBLK], none], axis=1), jnp.concatenate([none, q[QBLK:]], axis=1)], axis=0
+        )
+        sc = scores(q, jnp.concatenate(keys, axis=1))
+        w, total = softmax(jnp.where(jnp.concatenate(places, axis=0) < spare, sc, MASKED))
+        both = jnp.dot(w, jnp.concatenate(values, axis=1), preferred_element_type=jnp.float32)
+        read = jnp.concatenate([both[:QBLK, :HS], both[QBLK:, HS:]], axis=0)
+        mixed[rows, :] = gate * (read / total)
+        return c
 
     reach = WINDOW // tok
 
@@ -236,11 +250,11 @@
 
         return c
 
-    lax.fori_loop(0, reach, pass_halo, 0)
     to_slots.wait()
     arrived(qbuf, q_recv)
     arrived(membuf.at[1 - core, pl.ds(0, spare)], swap_recv)
-    lax.fori_loop(0, n_mem, mem_block, 0, unroll=2)
+    lax.fori_loop(0, n_mem // 2, mem_pair, 0, unroll=2)
+    lax.fori_loop(0, reach, pass_halo, 0)
 
     def take_rest(src, c):
         take(src)
@@ -297,9 +311,9 @@
 
     lax.fori_loop(0, batches // 2, local_batch, 0)
 
-    arrived(mem_dst_all(membuf, 0, (HEADS - 1) * half), mem_send)
-    arrived(mem_dst_all(membuf, 0, n_rank * half), z_send)
-    arrived(mem_dst_all(membuf, 0, spare), swap_send)
+    arrived(membuf.at[0, pl.ds(0, (HEADS - 1) * OWN)], mem_send)
+    arrived(membuf.at[0, pl.ds(0, n_rank * swapped)], z_send)
+    arrived(membuf.at[0, pl.ds(0, spare)], swap_send)
     arrived(qbuf.at[pl.ds(0, (n_mem - 1) * QBLK)], q_send)
     arrived(kvbuf.at[:, pl.ds(0, (n_mem - 1) * tok)], kv_send)
 
@@ -309,10 +323,6 @@
 
     arrived(obuf.at[pl.ds(0, (n_mem - 1) * QBLK)], out_send)
     arrived(out_ref, out_recv)
-
-
-def mem_dst_all(membuf, kind, count):
-    return membuf.at[kind, pl.ds(0, count)]
 
 
 def solution(mesh):

time: 47.4 us -> 44.2 us (0.932)
  the two profiles are of different devices: /device:TPU:37 before, /device:TPU:136 now
where the time goes in v4:
time: 44.2 us; the launch traced here: 44 us
  Pallas kernels  42.4 us (96%)
  local copies, waits for them, and re-layouts  1.67 us (4%)
    pallas_call x1, Pallas kernels, on_device(): pl.pallas_call(functools.partial(kernel, n_seq, n_mem, tok, shard), out_s...  42.4 us
    unnamed x1, local copies, waits for them, and re-layouts  1.67 us

profile of v4, /device:TPU:136, one launch (start us, length us, event | category | flops | bytes accessed | tf_op | source)
XLA Modules:
  0.0 44.0 jit_solution(5593483982788339392)
XLA Ops:
  0.0 42.4 %memorizing_attention.1 = bf16[128,1024]{1,0:T(8,128)(2,1)} custom-call(bf16[128,1024]{1,0:T(8,128)(2,1)} %q_ref.1, bf16[128,1024]{1,0:T(8,128)(2,1)} %k_ref.1, bf16[128,1024]{1,0:T(8,128)(2,1)} %v_ref.1, bf16[8,64,1024]{2,1,0:T(8,128)(2,1)} %bitcast.4, bf16[8,64,1024]{2,1,0:T(8,128)(2,1)} %bitcast.5, s32[8,32]{1,0:T(8,128)} %bitcast.6, s32[1,32]{1,0:T(1,128)} %bitcast.7, ...), custom_call_target="tpu_custom_call" | custom-call | tf_op jit(solution)/shard_map/memorizing_attention/pallas_call | solution.py:341
  42.4 1.7 %copy.11 = bf16[128,1024]{1,0:T(8,128)(2,1)} copy(bf16[128,1024]{1,0:T(8,128)(2,1)} %memorizing_attention.1) | data formatting | bytes 524288

commit v5 on v4

--- a/solution.py
+++ b/solution.py
@@ -160,6 +160,12 @@
         return c
 
 
+    early = (m >= n_mem - WINDOW // tok) | (m == 0)
+
+    @pl.when(early)
+    def _():
+        lax.fori_loop(0, n_mem - 1, send_kv, 0)
+
     for copy in smalls:
         copy.wait()
     named = [lists[j : j + 1, :] for j in range(LIST)]
@@ -181,7 +187,11 @@
         return c
 
     lax.fori_loop(0, n_rank, pass_first, 0)
-    lax.fori_loop(0, n_mem - 1, send_kv, 0)
+
+    @pl.when(jnp.logical_not(early))
+    def _():
+        lax.fori_loop(0, n_mem - 1, send_kv, 0)
+
 
     def pass_second(i, c):
         r = lax.rem(head + n_rank - i, n_rank)
@@ -253,8 +263,13 @@
     to_slots.wait()
     arrived(qbuf, q_recv)
     arrived(membuf.at[1 - core, pl.ds(0, spare)], swap_recv)
-    lax.fori_loop(0, n_mem // 2, mem_pair, 0, unroll=2)
-    lax.fori_loop(0, reach, pass_halo, 0)
+
+    def halo_and_mem(i, c):
+        pass_halo(i, c)
+        mem_pair(i, c)
+        return c
+
+    lax.fori_loop(0, reach, halo_and_mem, 0)
 
     def take_rest(src, c):
         take(src)
@@ -359,7 +374,7 @@
                 dma, dma((n_mem // 2,)), dma, dma((n_mem // 2,)), dma, dma, dma, dma,
             ],
             compiler_params=pltpu.CompilerParams(
-                collective_id=0, has_side_effects=True, vmem_limit_bytes=56 * 1024 * 1024
+                collective_id=0, has_side_effects=True, vmem_limit_bytes=107 * 512 * 1024
             ),
             name="memorizing_attention",
         )(q, k, v, by_block(mk), by_block(mv), lists, counts, docs, gate)

time: 44.2 us -> 43.5 us (0.984)
  the two profiles are of different devices: /device:TPU:136 before, /device:TPU:78 now
where the time goes in v5:
time: 43.5 us; the launch traced here: 43.3 us
  Pallas kernels  41.9 us (96%)
  local copies, waits for them, and re-layouts  1.39 us (3%)
    pallas_call x1, Pallas kernels, on_device(): pl.pallas_call(functools.partial(kernel, n_seq, n_mem, tok, shard), out_s...  41.9 us
    unnamed x9, local copies, waits for them, and re-layouts  1.39 us

profile of v5, /device:TPU:78, one launch (start us, length us, event | category | flops | bytes accessed | tf_op | source)
XLA Modules:
  0.0 43.3 jit_solution(9372577347501189886)
XLA Ops:
  0.0 0.0 copy-start
  0.0 0.0 copy-start.1
  0.0 0.0 copy-start.2
  0.0 0.0 copy-start.3
  0.0 0.7 %copy-done = s32[32,8]{0,1:T(8,128)S(1)} copy-done((s32[32,8]{0,1:T(8,128)S(1)}, s32[32,8]{0,1:T(8,128)}, u32[]{:S(2)}) %copy-start) | copy-done | bytes 1048
  0.7 0.0 copy-done.1
  0.7 0.0 copy-done.2
  0.7 0.0 copy-done.3
  0.7 41.9 %memorizing_attention.1 = bf16[128,1024]{1,0:T(8,128)(2,1)S(1)} custom-call(bf16[128,1024]{1,0:T(8,128)(2,1)} %q_ref.1, bf16[128,1024]{1,0:T(8,128)(2,1)} %k_ref.1, bf16[128,1024]{1,0:T(8,128)(2,1)} %v_ref.1, bf16[8,64,1024]{2,1,0:T(8,128)(2,1)} %bitcast.6, bf16[8,64,1024]{2,1,0:T(8,128)(2,1)} %bitcast.7, s32[8,32]{1,0:T(8,128)S(1)} %bitcast.4, ...), custom_call_target="tpu_custom_call" | custom-call | tf_op jit(solution)/shard_map/memorizing_attention/pallas_call | solution.py:356
  42.6 0.7 %copy.11 = bf16[128,1024]{1,0:T(8,128)(2,1)} copy(bf16[128,1024]{1,0:T(8,128)(2,1)S(1)} %memorizing_attention.1) | data formatting | bytes 524288
Async XLA Ops:
  0.0 0.7 %copy-start = (s32[32,8]{0,1:T(8,128)S(1)}, s32[32,8]{0,1:T(8,128)}, u32[]{:S(2)}) copy-start(s32[32,8]{0,1:T(8,128)} %param.14) | copy-start | bytes 3076
  0.0 0.7 %copy-start.1 = (s32[32]{0:T(128)S(1)}, s32[32]{0:T(128)}, u32[]{:S(2)}) copy-start(s32[32]{0:T(128)} %param.15) | copy-start | bytes 388
  0.0 0.7 %copy-start.2 = (s32[4]{0:T(128)S(1)}, s32[4]{0:T(128)}, u32[]{:S(2)}) copy-start(s32[4]{0:T(128)} %docs_ref.1) | copy-start | bytes 52
  0.0 0.7 %copy-start.3 = (f32[8]{0:T(128)S(1)}, f32[8]{0:T(128)}, u32[]{:S(2)}) copy-start(f32[8]{0:T(128)} %gate_ref.1) | copy-start | bytes 100

commit v6 on v5

--- a/solution.py
+++ b/solution.py
@@ -265,11 +265,13 @@
     arrived(membuf.at[1 - core, pl.ds(0, spare)], swap_recv)
 
     def halo_and_mem(i, c):
-        pass_halo(i, c)
-        mem_pair(i, c)
-        return c
-
-    lax.fori_loop(0, reach, halo_and_mem, 0)
+        pass_halo(2 * i, c)
+        pass_halo(2 * i + 1, c)
+        mem_pair(2 * i, c)
+        mem_pair(2 * i + 1, c)
+        return c
+
+    lax.fori_loop(0, reach // 2, halo_and_mem, 0)
 
     def take_rest(src, c):
         take(src)

time: 43.5 us -> 43.5 us (level)
  no operation moved by 1% of the time
where the time goes in v6:
time: 43.5 us; the launch traced here: 43.3 us
  Pallas kernels  41.9 us (96%)
  local copies, waits for them, and re-layouts  1.39 us (3%)
    pallas_call x1, Pallas kernels, on_device(): pl.pallas_call(functools.partial(kernel, n_seq, n_mem, tok, shard), out_s...  41.9 us
    unnamed x9, local copies, waits for them, and re-layouts  1.39 us

profile of v6, /device:TPU:78, one launch (start us, length us, event | category | flops | bytes accessed | tf_op | source)
XLA Modules:
  0.0 43.3 jit_solution(2093882451751308030)
XLA Ops:
  0.0 0.0 copy-start
  0.0 0.0 copy-start.1
  0.0 0.0 copy-start.2
  0.0 0.0 copy-start.3
  0.0 0.7 %copy-done = s32[32,8]{0,1:T(8,128)S(1)} copy-done((s32[32,8]{0,1:T(8,128)S(1)}, s32[32,8]{0,1:T(8,128)}, u32[]{:S(2)}) %copy-start) | copy-done | bytes 1048
  0.7 0.0 copy-done.1
  0.7 0.0 copy-done.2
  0.7 0.0 copy-done.3
  0.7 41.9 %memorizing_attention.1 = bf16[128,1024]{1,0:T(8,128)(2,1)S(1)} custom-call(bf16[128,1024]{1,0:T(8,128)(2,1)} %q_ref.1, bf16[128,1024]{1,0:T(8,128)(2,1)} %k_ref.1, bf16[128,1024]{1,0:T(8,128)(2,1)} %v_ref.1, bf16[8,64,1024]{2,1,0:T(8,128)(2,1)} %bitcast.6, bf16[8,64,1024]{2,1,0:T(8,128)(2,1)} %bitcast.7, s32[8,32]{1,0:T(8,128)S(1)} %bitcast.4, ...), custom_call_target="tpu_custom_call" | custom-call | tf_op jit(solution)/shard_map/memorizing_attention/pallas_call | solution.py:358
  42.6 0.7 %copy.11 = bf16[128,1024]{1,0:T(8,128)(2,1)} copy(bf16[128,1024]{1,0:T(8,128)(2,1)S(1)} %memorizing_attention.1) | data formatting | bytes 524288
Async XLA Ops:
  0.0 0.7 %copy-start = (s32[32,8]{0,1:T(8,128)S(1)}, s32[32,8]{0,1:T(8,128)}, u32[]{:S(2)}) copy-start(s32[32,8]{0,1:T(8,128)} %param.14) | copy-start | bytes 3076
  0.0 0.7 %copy-start.1 = (s32[32]{0:T(128)S(1)}, s32[32]{0:T(128)}, u32[]{:S(2)}) copy-start(s32[32]{0:T(128)} %param.15) | copy-start | bytes 388
  0.0 0.7 %copy-start.2 = (s32[4]{0:T(128)S(1)}, s32[4]{0:T(128)}, u32[]{:S(2)}) copy-start(s32[4]{0:T(128)} %docs_ref.1) | copy-start | bytes 52
  0.0 0.7 %copy-start.3 = (f32[8]{0:T(128)S(1)}, f32[8]{0:T(128)}, u32[]{:S(2)}) copy-start(f32[8]{0:T(128)} %gate_ref.1) | copy-start | bytes 100
